TPU v7x, 512 devices: a whole 4x8x8 slice. The times are simulated.
512 devices in a mesh: gz: 16 (over y, core), gy: 32 (over x, z).
Axes of the slice: x: 4, y: 8, z: 8, core: 2. Of those that a mesh axis runs over, the one named last changes fastest.
Arguments:
- field: bfloat16 [8, 512, 64, 2048], P(None, 'gy', None, 'gz'), may hold values from -6 to 6
- spectral_weight: bfloat16 [64, 32, 2, 64, 64], P('gy', None, None, 'gz'), may hold values from -4 to 4
- local_weight: bfloat16 [64, 64], replicated, may hold values from -0.75 to 0.75
- bias: bfloat16 [64], replicated, may hold values from -3 to 3
Outputs:
- mixed: bfloat16 [8, 512, 64, 2048], P(None, 'gy', None, 'gz')
All inputs are finite; a program needn't handle non-finite values.
Results may differ from a plain program's by a relative error of at most 0.017.
Values may be sent and summed in bfloat16 or wider, within the bound.
A program may use at most 64 MiB of HBM per device.

v0:
```python
import math

import jax
import jax.numpy as jnp
from jax import lax
from jax.sharding import PartitionSpec as P


def phase_of(first, second, modulus):
    return (first * second % modulus).astype(jnp.float32) * (2.0 * math.pi / modulus)


def gelu_tanh(value):
    return 0.5 * value * (1.0 + jnp.tanh(0.7978845608 * (value + 0.044715 * value * value * value)))


def on_device(field, spectral_weight, local_weight, bias):
    highest = lax.Precision.HIGHEST
    plane_count, row_count, channels, depth = field.shape
    band_ky = spectral_weight.shape[0]
    modes_z = spectral_weight.shape[1]
    total_y = row_count * lax.axis_size("gy")
    total_z = depth * lax.axis_size("gz")
    ky_total = band_ky * lax.axis_size("gy")
    ky_side = ky_total // 2
    band_kz = modes_z // lax.axis_size("gz")
    y_global = lax.axis_index("gy") + lax.axis_size("gy") * jnp.arange(row_count, dtype=jnp.int32)
    z_global = lax.axis_index("gz") + lax.axis_size("gz") * jnp.arange(depth, dtype=jnp.int32)
    kz_index = jnp.arange(lax.axis_size("gz") * band_kz, dtype=jnp.int32)
    z_phase = phase_of(z_global[:, None], kz_index[None, :], total_z)
    z_table = jnp.stack([jnp.cos(z_phase), -jnp.sin(z_phase)], -1).astype(jnp.bfloat16)
    partial_modes = jnp.einsum(
        "xycz,zkp->kxypc", field, z_table, preferred_element_type=jnp.float32
    )
    zmodes = lax.psum_scatter(
        partial_modes.reshape(
            lax.axis_size("gz") * band_kz, plane_count, row_count, 2 * channels
        ).astype(jnp.bfloat16),
        "gz",
        scatter_dimension=0,
        tiled=True,
    ).astype(jnp.float32)
    z_real = zmodes[..., :channels]
    z_imag = zmodes[..., channels:]

    def y_tables(count):
        ky_index = jnp.arange(count, dtype=jnp.int32)
        wavenum = jnp.where(ky_index < ky_side, ky_index, ky_index + total_y - 2 * ky_side)
        y_phase = phase_of(wavenum[:, None], y_global[None, :], total_y)
        return (jnp.cos(y_phase).astype(jnp.bfloat16), jnp.sin(y_phase).astype(jnp.bfloat16))

    cosine_table, sine_table = y_tables(lax.axis_size("gy") * band_ky)
    cosine_table = cosine_table.astype(jnp.float32)
    sine_table = sine_table.astype(jnp.float32)
    spec_real = jnp.einsum("jy,kxyc->jkxc", cosine_table, z_real, precision=highest) + jnp.einsum(
        "jy,kxyc->jkxc", sine_table, z_imag, precision=highest
    )
    spec_imag = jnp.einsum("jy,kxyc->jkxc", cosine_table, z_imag, precision=highest) - jnp.einsum(
        "jy,kxyc->jkxc", sine_table, z_real, precision=highest
    )
    spectrum = lax.psum_scatter(
        jnp.concatenate([spec_real, spec_imag], -1).astype(jnp.bfloat16),
        "gy",
        scatter_dimension=0,
        tiled=True,
    ).astype(jnp.float32)
    full_weight = lax.all_gather(spectral_weight, "gz", axis=3, tiled=True)
    band_weight = lax.dynamic_slice_in_dim(full_weight, lax.axis_index("gz") * band_kz, band_kz, 1)
    band_weight = band_weight.astype(jnp.float32)
    weight_real = band_weight[:, :, 0]
    weight_imag = band_weight[:, :, 1]
    upper_block = jnp.concatenate([weight_real, weight_imag], -1)
    lower_block = jnp.concatenate([-weight_imag, weight_real], -1)
    complex_block = jnp.concatenate([upper_block, lower_block], -2)
    product = jnp.einsum("jkxi,jkio->jkxo", spectrum, complex_block, precision=highest).astype(
        jnp.bfloat16
    )
    all_bands = lax.all_gather(product, "gz", axis=1, tiled=True)
    piece = lax.all_gather(all_bands, "gy", axis=0, tiled=True)
    cosine_table, sine_table = y_tables(piece.shape[0])
    prod_real = piece[..., :channels]
    prod_imag = piece[..., channels:]
    rows_real = jnp.einsum(
        "jy,jkxo->kxyo", cosine_table, prod_real, preferred_element_type=jnp.float32
    ) - jnp.einsum("jy,jkxo->kxyo", sine_table, prod_imag, preferred_element_type=jnp.float32)
    rows_imag = jnp.einsum(
        "jy,jkxo->kxyo", sine_table, prod_real, preferred_element_type=jnp.float32
    ) + jnp.einsum("jy,jkxo->kxyo", cosine_table, prod_imag, preferred_element_type=jnp.float32)
    rows_back = jnp.concatenate([rows_real, rows_imag], -1).astype(jnp.bfloat16)
    kz_index = jnp.arange(modes_z, dtype=jnp.int32)
    doubling = jnp.where(kz_index == 0, 1.0, 2.0).astype(jnp.float32)
    back_phase = phase_of(kz_index[:, None], z_global[None, :], total_z)
    back_table = jnp.stack(
        [doubling[:, None] * jnp.cos(back_phase), -(doubling[:, None] * jnp.sin(back_phase))], 1
    ).astype(jnp.bfloat16)
    rows_pair = rows_back.reshape(modes_z, plane_count, row_count, 2, channels)
    spectral = jnp.einsum(
        "kpz,kxypc->xycz", back_table, rows_pair, preferred_element_type=jnp.float32
    ) / float(total_y * total_z)
    linear = jnp.einsum("oc,xycz->xyoz", local_weight, field, preferred_element_type=jnp.float32)
    offset = bias.astype(jnp.float32)[None, None, :, None]
    return gelu_tanh(spectral + linear + offset).astype(jnp.bfloat16)


def solution(mesh):
    return jax.shard_map(
        on_device,
        mesh=mesh,
        in_specs=(P(None, "gy", None, "gz"), P("gy", None, None, "gz", None), P(), P()),
        out_specs=P(None, "gy", None, "gz"),
        check_vma=False,
    )
```

profile of v0, /device:TPU:1, one launch (start us, length us, event | category | flops | bytes accessed | tf_op | source)
XLA Modules:
  0.0 471.4 jit_solution(2276012895792037780)
XLA Ops:
  6.5 0.0 copy-start
  6.5 0.0 all-gather.3.cloned.1.call-start
  6.5 1.7 copy.27
  8.3 0.0 all-gather.3.cloned.1.call-update
  8.3 0.0 reduce-scatter.3.cloned.1.call-start
  8.3 0.1 cosine_convert_fusion
  8.4 0.0 copy-done
  8.5 2.1 convert_bitcast_fusion
  10.6 3.5 copy.25
  14.1 4.8 %convert_element_type.75 = bf16[32,8,16,128]{3,2,1,0:T(8,128)(2,1)} reshape(bf16[32,8,16,2,64]{4,3,2,1,0:T(2,128)(2,1)} %copy.25) | data formatting | bytes 2097152 | tf_op jit(solution)/shard_map/convert_element_type | solution.py:38
  18.8 0.0 copy-start.2
  18.8 0.0 reduce-scatter.3.cloned.1.call-update
  18.8 0.0 reduce-scatter.5.cloned.1.call-start
  18.9 38.4 %all-gather.3.cloned.1.call-done = bf16[2,32,2,64,64]{4,1,2,0,3:T(8,128)(2,1)} async-done(((bf16[2,32,2,4,64]{4,1,2,0,3:T(8,128)(2,1)}), bf16[2,32,2,64,64]{4,1,2,0,3:T(8,128)(2,1)}) %all-gather.3.cloned.1.call-update) | async-done | bytes 1048592 | tf_op jit(solution)/shard_map/all_gather | solution.py:67
  57.3 1.2 constant_dynamic-slice_fusion
  58.5 58.2 %reduce-scatter.3.cloned.1.call-done = bf16[2,8,16,128]{3,2,1,0:T(8,128)(2,1)} async-done(((bf16[32,8,16,128]{3,2,1,0:T(8,128)(2,1)}), bf16[2,8,16,128]{3,2,1,0:T(8,128)(2,1)}) %reduce-scatter.3.cloned.1.call-update) | async-done | bytes 65552 | tf_op jit(solution)/shard_map/reduce_scatter | solution.py:35
  116.7 1.2 fusion.43
  117.9 1.2 fusion.39
  119.1 1.2 fusion.30
  120.3 1.2 fusion.31
  121.6 0.2 pad_maximum_fusion.1
  121.7 0.9 copy.26
  122.6 0.0 reduce-scatter.5.cloned.1.call-update
  122.6 0.0 all-gather.5.cloned.1.call-start
  122.7 214.8 %reduce-scatter.5.cloned.1.call-done = bf16[2,2,8,128]{3,2,1,0:T(8,128)(2,1)} async-done(((bf16[64,2,8,128]{3,2,1,0:T(8,128)(2,1)}), bf16[2,2,8,128]{3,2,1,0:T(8,128)(2,1)}) %reduce-scatter.5.cloned.1.call-update) | async-done | bytes 8208 | tf_op jit(solution)/shard_map/reduce_scatter | solution.py:61
  337.6 1.0 convolution_convert_fusion
  338.6 24.3 %all_gather.10 = bf16[2,32,8,128]{3,2,1,0:T(8,128)(2,1)} all-gather(bf16[2,2,8,128]{3,2,1,0:T(8,128)(2,1)S(1)} %convolution_convert_fusion), channel_id=1, replica_groups=mesh['gz'=16,'gy'=32] {'gz'}, dimensions={1}, use_global_device_ids=true | all-gather | bytes 139264 | tf_op jit(solution)/shard_map/all_gather | solution.py:78
  362.9 0.0 all-gather.5.cloned.1.call-update
  362.9 0.0 copy-done.2
  363.0 0.1 multiply_convert_fusion
  363.1 80.2 %all-gather.5.cloned.1.call-done = bf16[64,32,8,128]{3,2,1,0:T(8,128)(2,1)} async-done(((bf16[2,32,8,128]{3,2,1,0:T(8,128)(2,1)}), bf16[64,32,8,128]{3,2,1,0:T(8,128)(2,1)}) %all-gather.5.cloned.1.call-update) | async-done | bytes 4194320 | tf_op jit(solution)/shard_map/all_gather | solution.py:79
  443.3 5.1 %fusion.111 = (bf16[64,32,8,64]{3,2,1,0:T(8,128)(2,1)S(1)}, bf16[64,32,8,64]{3,2,1,0:T(8,128)(2,1)S(1)}) fusion(bf16[64,32,8,128]{3,2,1,0:T(8,128)(2,1)} %all-gather.5.cloned.1.call-done), kind=kLoop, calls=%fused_computation.131 | loop fusion | bytes 8388608 | tf_op jit(solution)/shard_map/slice | solution.py:81
  448.4 2.4 fusion.6
  450.8 2.4 fusion.8
  453.3 2.6 fusion.24
  455.8 2.6 fusion.27
  458.4 0.5 pad_maximum_fusion
  458.9 0.0 copy-start.1
  458.9 2.4 fusion.16
  461.3 0.0 copy-done.1
  461.3 3.5 fusion.4
  (8 shorter events, 0.1 us)
Async XLA Ops:
  6.5 1.9 copy-start
  6.5 50.8 %all-gather.3.cloned.1.call-start = ((), (), s32[]{:S(2)}) async-start(), calls=%async_computation.4 | async-start | bytes 2228224 | tf_op jit(solution)/shard_map/all_gather | solution.py:67
  8.3 108.4 %reduce-scatter.3.cloned.1.call-start = ((), (), s32[]{:S(2)}) async-start(), calls=%async_computation.2 | async-start | bytes 1114112 | tf_op jit(solution)/shard_map/reduce_scatter | solution.py:35
  18.8 344.1 %copy-start.2 = (bf16[64]{0:T(256)(128)(2,1)S(1)}, bf16[64]{0:T(256)(128)(2,1)}, u32[]{:S(2)}) copy-start(bf16[64]{0:T(256)(128)(2,1)} %param.7) | copy-start | bytes 388
  18.8 318.7 %reduce-scatter.5.cloned.1.call-start = ((), (), s32[]{:S(2)}) async-start(), calls=%async_computation.3 | async-start | bytes 270336 | tf_op jit(solution)/shard_map/reduce_scatter | solution.py:61
  122.6 320.7 %all-gather.5.cloned.1.call-start = ((), (), s32[]{:S(2)}) async-start(), calls=%async_computation.5 | async-start | bytes 4325376 | tf_op jit(solution)/shard_map/all_gather | solution.py:79
  458.9 2.4 copy-start.1
Sparse Core Ops, SparseCore 0:
  9.5 47.7 all-gather.2
  60.1 56.5 reduce-scatter.2
  122.7 214.7 reduce-scatter.4
  363.1 80.1 all-gather.4
where the time goes:
time: 474 us; the launch traced here: 471 us
  waiting for transfers between devices  392 us (83%)
  blocking collectives  24.3 us (5%)
  matrix products  23.9 us (5%)
  local copies, waits for them, and re-layouts  17.2 us (4%)
  between operations  13.3 us (3%)
    reduce_scatter x1, waiting for transfers between devices, on_device(): lax.psum_scatter(jnp.concatenate([spec_real, spec_imag], -1).astype(jnp.b...  215 us
    all_gather x1, waiting for transfers between devices, on_device(): piece = lax.all_gather(all_bands, 'gy', axis=0, tiled=True)  80.2 us
    reduce_scatter x1, waiting for transfers between devices, on_device(): lax.psum_scatter(partial_modes.reshape(lax.axis_size('gz') * band_kz, pla...  58.2 us
    all_gather x1, waiting for transfers between devices, on_device(): full_weight = lax.all_gather(spectral_weight, 'gz', axis=3, tiled=True)  38.4 us
    all_gather x1, blocking collectives, on_device(): all_bands = lax.all_gather(product, 'gz', axis=1, tiled=True)  24.3 us
  transfers between devices with their start and end apart: 4, of which 4 were waited for; matrix products, arithmetic and copies ran while one was open for 3% of the time, Pallas kernels for 0%

commit v1 on v0

v1 whole, which is shorter than its diff:
```python
import functools
import math

import jax
import jax.numpy as jnp
import ml_dtypes
import numpy as np
from jax import lax
from jax.experimental import pallas as pl
from jax.experimental.pallas import tpu as pltpu
from jax.sharding import PartitionSpec as P

MESH = pl.DeviceIdType.MESH
BF16 = jnp.bfloat16
F32 = jnp.float32
CHUNKS = 2


def phase_of(number, modulus):
    return (number % modulus).astype(np.float32) * np.float32(2.0 * math.pi / modulus)


def rounded(array):
    return np.asarray(array, np.float32).astype(ml_dtypes.bfloat16).astype(np.float32)


def z_tables(ring, depth):
    size = 2 * ring
    cell = np.arange(depth)
    tables = []
    for d in range(size):
        owner = np.array(
            [((d // 2 + t) % ring) * 2 + (d % 2 ^ r) for r in range(2) for t in range(ring)]
        )
        mode = owner[:, None] * 2 + np.arange(2)
        angle = phase_of(mode[:, :, None] * (cell * size + d), depth * size)
        base = np.stack([np.cos(angle), -np.sin(angle)], 2)
        tables.append(np.repeat(base[:, None], 4, 1).reshape(size * 16, depth))
    return rounded(np.stack(tables))


def y_tables(nx, nz, rows):
    size = nx * nz
    total = rows * size
    forward, back = [], []
    for e in range(size):
        owner = np.array(
            [((e // nz + a) % nx) * nz + (e % nz + b) % nz for a in range(nx) for b in range(nz)]
        )
        mode = owner[:, None] * 2 + np.arange(2)
        wave = np.where(mode < size, mode, mode + total - 2 * size)
        angle = phase_of(wave[:, :, None] * (np.arange(rows) * size + e), total)
        cosine, sine = np.cos(angle), np.sin(angle)
        there = np.stack([np.stack([cosine, sine], -1), np.stack([-sine, cosine], -1)], 2)
        there = np.einsum("ujqyp,kl->ujkqylp", there, np.eye(2))
        forward.append(there.reshape(size * 8, rows * 4))
        here = np.stack([np.stack([cosine, -sine], -1), np.stack([sine, cosine], -1)], 2)
        here = np.einsum("ujqyp,kl->ykqujlp", here, np.eye(2))
        back.append(here.reshape(rows * 4, size * 8))
    return rounded(np.stack(forward)), rounded(np.stack(back))


def gelu_tanh(value):
    return 0.5 * value * (1.0 + jnp.tanh(0.7978845608 * (value + 0.044715 * value * value * value)))


def split(value):
    high = value.astype(BF16)
    return high, (value - high.astype(F32)).astype(BF16)


def dot(left, right, dims=((1,), (0,))):
    return lax.dot_general(left, right, (dims, ((), ())), preferred_element_type=F32)


def kernel(
    geometry, scale,
    field, weight, pointwise, bias, table_z, table_f, table_b, out,
    fv, wv, tz, tf, tb, acc, sib_out, sib_in, a_out, a_in, b_out, b_in, c_in, d_in,
    w_mess, w_out, w_in, w_stage, w_full, small, wide, lin,
    local, local_f, local_w, sib_s, sib_r, a_s, a_r, b_s, b_r, c_s, c_r, d_s, d_r, e_s, e_r, w_s, w_r,
):
    ring, nx, nz, planes, rows, channels, depth = geometry
    gz, gy = 2 * ring, nx * nz
    per = planes // CHUNKS
    lanes = per * channels
    half = lanes // 2
    groups = rows // 4
    band = channels // gz
    d = lax.axis_index("gz")
    e = lax.axis_index("gy")
    core = lax.rem(d, 2)

    def chip(t):
        return {"gz": lax.rem(d + 2 * t, gz)}

    sibling = {"gz": d + 1 - 2 * core}
    ex, ez = e // nz, lax.rem(e, nz)

    def plane(a, b):
        return {"gy": lax.rem(ex + a, nx) * nz + lax.rem(ez + b, nz)}

    partners = [(a, b) for a in range(nx) for b in range(nz)][1:]

    def slot(a, b):
        return ((nx - a) % nx) * nz + (nz - b) % nz

    def remote(src, dst, send, recv, device):
        return pltpu.make_async_remote_copy(
            src_ref=src, dst_ref=dst, send_sem=send, recv_sem=recv, device_id=device, device_id_type=MESH
        )

    get_tz = pltpu.make_async_copy(table_z.at[d], tz, local.at[0])
    get_f = [
        pltpu.make_async_copy(
            field.at[pl.ds(ch * per, per)], fv.at[pl.ds(ch * per, per)], local_f.at[ch]
        )
        for ch in range(CHUNKS)
    ]
    get_w = pltpu.make_async_copy(weight, wv, local.at[1])
    get_tf = pltpu.make_async_copy(table_f.at[e], tf, local.at[2])
    get_tb = pltpu.make_async_copy(table_b.at[e], tb, local.at[3])
    get_tz.start()
    for copy in get_f:
        copy.start()
    get_w.start()
    get_tf.start()
    get_tb.start()

    barrier = pltpu.get_barrier_semaphore()
    for step in range(1, gz):
        pl.semaphore_signal(
            barrier, inc=1, device_id={"gz": lax.rem(d + step, gz)}, device_id_type=MESH
        )
    for a, b in partners:
        pl.semaphore_signal(barrier, inc=1, device_id=plane(a, b), device_id_type=MESH)
    pl.semaphore_wait(barrier, gz - 1 + gy - 1)

    get_tz.wait()
    member = lax.rem(lax.broadcasted_iota(jnp.int32, (gz * 16, depth), 0) // 4, 4)
    table = jnp.concatenate(
        [jnp.where(member == i, tz[...], 0.0).astype(BF16) for i in range(4)], axis=1
    )
    own_rows = ring * 16
    for ch in range(CHUNKS):
        get_f[ch].wait()
        for g in range(groups):
            cells = jnp.concatenate(
                [
                    fv[ch * per : (ch + 1) * per, g * 4 + i].reshape(lanes, depth)
                    for i in range(4)
                ],
                axis=1,
            )
            part = dot(table, cells, ((1,), (1,)))
            sib_out[ch, g] = part[own_rows:].astype(BF16)
            acc[ch, g] = part[:own_rows]
            remote(
                sib_out.at[ch, g], sib_in.at[ch, g], sib_s.at[ch, g], sib_r.at[ch, g], sibling
            ).start()

    for ch in range(CHUNKS):
        for g in range(groups):
            remote(
                sib_out.at[ch, g], sib_in.at[ch, g], sib_s.at[ch, g], sib_r.at[ch, g], sibling
            ).wait_recv()
            total = acc[ch, g] + sib_in[ch, g].astype(F32)
            acc[ch, g, 0:16] = total[0:16]
            for t in range(1, ring):
                a_out[ch, t - 1, g * 16 : (g + 1) * 16] = total[t * 16 : (t + 1) * 16].astype(BF16)
        for t in range(1, ring):
            remote(
                a_out.at[ch, t - 1], a_in.at[ch, ring - 1 - t], a_s.at[ch], a_r.at[ch], chip(t)
            ).start()

    get_w.wait()
    for jj in range(2):
        for k in range(2 * gz):
            for p in range(2):
                row = (jj * 2 + k % 2) * band
                w_mess[k // 2, row : row + band, p * channels : (p + 1) * channels] = wv[
                    jj, k, p
                ].astype(F32)
    w_out[...] = w_mess[...].astype(BF16)
    own_w = pltpu.make_async_copy(w_out.at[d], w_in.at[d], local_w)
    own_w.start()
    for step in range(1, gz):
        dest = lax.rem(d + step, gz)
        remote(w_out.at[dest], w_in.at[d], w_s, w_r, {"gz": dest}).start()

    block = per * channels
    row_id = lax.broadcasted_iota(jnp.int32, (block, block), 0) // channels
    col_id = lax.broadcasted_iota(jnp.int32, (block, block), 1) // channels
    row = jnp.concatenate([pointwise[...].astype(F32)] * per, axis=1)
    mixing = jnp.where(row_id == col_id, jnp.concatenate([row] * per, axis=0), 0.0).astype(BF16)
    first = lax.broadcasted_iota(jnp.int32, (block, channels), 0)
    second = lax.broadcasted_iota(jnp.int32, (block, channels), 1)
    pick = jnp.where(
        lax.rem(first, channels) == second, jnp.broadcast_to(bias[...].astype(F32), (block, channels)), 0.0
    ).astype(BF16)
    offset = dot(pick, jnp.ones((channels, 4 * depth), BF16))
    for ch in range(CHUNKS):
        for g in range(groups):
            cells = jnp.concatenate(
                [
                    fv[ch * per : (ch + 1) * per, g * 4 + i].reshape(lanes, depth)
                    for i in range(4)
                ],
                axis=1,
            )
            lin[ch, g] = dot(mixing, cells) + offset

    get_tf.wait()
    ahead = tf[...].astype(BF16)
    ahead = jnp.concatenate([ahead, ahead], axis=1)
    for ch in range(CHUNKS):
        remote(a_in.at[ch], a_in.at[ch], a_s.at[ch], a_r.at[ch], chip(1)).wait_recv()
        modes = jnp.concatenate([acc[ch, g, 0:16] for g in range(groups)], axis=0)
        for t in range(ring - 1):
            modes = modes + a_in[ch, t].astype(F32)
        high, low = split(modes)
        part = dot(ahead, jnp.concatenate([high, low], axis=0))
        part = part.reshape(gy, 8, lanes)
        b_out[ch] = jnp.concatenate([part[:, :, :half], part[:, :, half:]], axis=1).astype(BF16)
        b_in[ch, 0] = b_out[ch, 0]
        for a, b in partners:
            remote(
                b_out.at[ch, a * nz + b], b_in.at[ch, slot(a, b)], b_s.at[ch], b_r.at[ch], plane(a, b)
            ).start()

    own_w.wait()
    remote(w_in.at[pl.ds(0, gz - 1)], w_in.at[pl.ds(0, gz - 1)], w_s, w_r, chip(1)).wait_recv()
    w_mess[...] = w_in[...].astype(F32)
    for source in range(gz):
        for jk in range(4):
            w_stage[jk, source * band : (source + 1) * band] = w_mess[
                source, jk * band : (jk + 1) * band
            ]
    sign = jnp.where(
        lax.broadcasted_iota(jnp.int32, (channels, 2 * channels), 1) < channels, -1.0, 1.0
    )
    for jk in range(4):
        upper = w_stage[jk]
        lower = pltpu.roll(upper, channels, 1) * sign
        w_full[jk] = jnp.concatenate([upper, lower], axis=0).astype(BF16)

    per_half = per // 2
    for ch in range(CHUNKS):
        remote(
            b_in.at[ch, pl.ds(1, gy - 1)], b_in.at[ch, pl.ds(1, gy - 1)], b_s.at[ch], b_r.at[ch], plane(0, 1)
        ).wait_recv()
        spectrum = jnp.sum(b_in[ch].astype(F32), axis=0)
        for h in range(half // 128):
            small[h] = spectrum[:, h * 128 : (h + 1) * 128]
        for h in range(half // 128):
            real = small[h, pl.ds(0, 8, stride=2), :]
            imag = small[h, pl.ds(1, 8, stride=2), :]
            for s in range(128 // channels):
                lane = s * channels
                x = h * (128 // channels) + s
                wide[x * 8 : (x + 1) * 8, :] = jnp.concatenate(
                    [real[:, lane : lane + channels], imag[:, lane : lane + channels]], axis=1
                )
        products = []
        for jk in range(4):
            high, low = split(wide[pl.ds(jk, 2 * per_half, stride=4), :])
            both = dot(jnp.concatenate([high, low], axis=0), w_full[jk])
            products.append(both[: 2 * per_half] + both[2 * per_half :])
        for jk in range(4):
            wide[pl.ds(jk, 2 * per_half, stride=4), :] = products[jk]
        for h in range(half // 128):
            pieces = [
                wide[(h * (128 // channels) + s) * 8 : (h * (128 // channels) + s + 1) * 8, :]
                for s in range(128 // channels)
            ]
            small[h, pl.ds(0, 8, stride=2), :] = jnp.concatenate(
                [piece[:, :channels] for piece in pieces], axis=1
            )
            small[h, pl.ds(1, 8, stride=2), :] = jnp.concatenate(
                [piece[:, channels:] for piece in pieces], axis=1
            )
        c_in[ch, 0] = jnp.concatenate([small[h] for h in range(half // 128)], axis=1).astype(BF16)
        for a, b in partners:
            remote(
                c_in.at[ch, 0], c_in.at[ch, slot(a, b)], c_s.at[ch], c_r.at[ch], plane(a, b)
            ).start()

    get_tb.wait()
    behind = tb[...].astype(BF16)
    line = lax.broadcasted_iota(jnp.int32, (rows * 4, lanes), 0)
    low_mode = jnp.logical_and(lax.rem(line, 4) < 2, d == 0)
    factor = jnp.where(low_mode, scale, 2.0 * scale)
    for ch in range(CHUNKS):
        remote(
            c_in.at[ch, pl.ds(1, gy - 1)], c_in.at[ch, pl.ds(1, gy - 1)], c_s.at[ch], c_r.at[ch], plane(0, 1)
        ).wait_recv()
        bands = c_in[ch].astype(F32)
        bands = jnp.concatenate([bands[:, 0:8], bands[:, 8:16]], axis=2)
        bands = bands.reshape(gy * 8, lanes).astype(BF16)
        d_in[ch, 0, 0] = (dot(behind, bands) * factor).astype(BF16)
        remote(d_in.at[ch, 0, 0], d_in.at[ch, 1, 0], e_s.at[ch, 0], e_r.at[ch, 0], sibling).start()
        for t in range(1, ring):
            remote(
                d_in.at[ch, 0, 0], d_in.at[ch, 0, ring - t], d_s.at[ch], d_r.at[ch, ring - t], chip(t)
            ).start()

    order = sorted(range(1, ring), key=lambda t: min(t, ring - t))
    for ch in range(CHUNKS):
        for t in order:
            remote(
                d_in.at[ch, 0, 0], d_in.at[ch, 0, t], d_s.at[ch], d_r.at[ch, t], chip(1)
            ).wait_recv()
            remote(
                d_in.at[ch, 0, t], d_in.at[ch, 1, t], e_s.at[ch, t], e_r.at[ch, t], sibling
            ).start()
        for t in [0] + order:
            remote(
                d_in.at[ch, 0, t], d_in.at[ch, 1, t], e_s.at[ch, t], e_r.at[ch, t], sibling
            ).wait_recv()
        for g in range(groups):
            spectral = d_in[ch, :, :, g * 16 : (g + 1) * 16].reshape(gz * 16, lanes)
            value = gelu_tanh(dot(spectral, table, ((0,), (0,))) + lin[ch, g])
            value = value.astype(BF16).reshape(per, channels, 4 * depth)
            for i in range(4):
                out[ch * per : (ch + 1) * per, g * 4 + i] = value[:, :, i * depth : (i + 1) * depth]

    for ch in range(CHUNKS):
        for g in range(groups):
            remote(
                sib_out.at[ch, g], sib_in.at[ch, g], sib_s.at[ch, g], sib_r.at[ch, g], sibling
            ).wait_send()
        remote(a_out.at[ch], a_in.at[ch], a_s.at[ch], a_r.at[ch], chip(1)).wait_send()
        remote(
            b_out.at[ch, pl.ds(1, gy - 1)], b_in.at[ch, pl.ds(1, gy - 1)], b_s.at[ch], b_r.at[ch], plane(0, 1)
        ).wait_send()
        remote(
            c_in.at[ch, pl.ds(1, gy - 1)], c_in.at[ch, pl.ds(1, gy - 1)], c_s.at[ch], c_r.at[ch], plane(0, 1)
        ).wait_send()
        remote(
            d_in.at[ch, 0, pl.ds(1, ring - 1)], d_in.at[ch, 0, pl.ds(1, ring - 1)], d_s.at[ch], d_r.at[ch, 1], chip(1)
        ).wait_send()
        for t in range(ring):
            remote(
                d_in.at[ch, 0, t], d_in.at[ch, 1, t], e_s.at[ch, t], e_r.at[ch, t], sibling
            ).wait_send()
    remote(w_in.at[pl.ds(0, gz - 1)], w_in.at[pl.ds(0, gz - 1)], w_s, w_r, chip(1)).wait_send()


def on_device(ring, nx, nz, field, spectral_weight, local_weight, bias):
    planes, rows, channels, depth = field.shape
    gz, gy = 2 * ring, nx * nz
    geometry = (ring, nx, nz, planes, rows, channels, depth)
    scale = 1.0 / (rows * gy * depth * gz)
    forward, back = y_tables(nx, nz, rows)
    table_z = z_tables(ring, depth)
    per = planes // CHUNKS
    lanes = per * channels
    half = lanes // 2
    groups = rows // 4
    band = channels // gz
    dma = pltpu.SemaphoreType.DMA
    scratch = [
        pltpu.VMEM(field.shape, BF16),
        pltpu.VMEM(spectral_weight.shape, BF16),
        pltpu.VMEM(table_z.shape[1:], F32),
        pltpu.VMEM(forward.shape[1:], F32),
        pltpu.VMEM(back.shape[1:], F32),
        pltpu.VMEM((CHUNKS, groups, ring * 16, lanes), F32),
        pltpu.VMEM((CHUNKS, groups, ring * 16, lanes), BF16),
        pltpu.VMEM((CHUNKS, groups, ring * 16, lanes), BF16),
        pltpu.VMEM((CHUNKS, ring - 1, rows * 4, lanes), BF16),
        pltpu.VMEM((CHUNKS, ring - 1, rows * 4, lanes), BF16),
        pltpu.VMEM((CHUNKS, gy, 16, half), BF16),
        pltpu.VMEM((CHUNKS, gy, 16, half), BF16),
        pltpu.VMEM((CHUNKS, gy, 16, half), BF16),
        pltpu.VMEM((CHUNKS, 2, ring, rows * 4, lanes), BF16),
        pltpu.VMEM((gz, 4 * band, 2 * channels), F32),
        pltpu.VMEM((gz, 4 * band, 2 * channels), BF16),
        pltpu.VMEM((gz, 4 * band, 2 * channels), BF16),
        pltpu.VMEM((4, channels, 2 * channels), F32),
        pltpu.VMEM((4, 2 * channels, 2 * channels), BF16),
        pltpu.VMEM((half // 128, 16, 128), F32),
        pltpu.VMEM((per * 4, 2 * channels), F32),
        pltpu.VMEM((CHUNKS, groups, lanes, 4 * depth), F32),
        dma((4,)), dma((CHUNKS,)), dma,
        dma((CHUNKS, groups)), dma((CHUNKS, groups)),
        dma((CHUNKS,)), dma((CHUNKS,)),
        dma((CHUNKS,)), dma((CHUNKS,)),
        dma((CHUNKS,)), dma((CHUNKS,)),
        dma((CHUNKS,)), dma((CHUNKS, ring)),
        dma((CHUNKS, ring)), dma((CHUNKS, ring)),
        dma, dma,
    ]
    anywhere = pl.BlockSpec(memory_space=pltpu.HBM)
    vmem = pl.BlockSpec(memory_space=pltpu.VMEM)
    return pl.pallas_call(
        functools.partial(kernel, geometry, scale),
        out_shape=jax.ShapeDtypeStruct(field.shape, BF16),
        in_specs=[anywhere, anywhere, vmem, vmem, anywhere, anywhere, anywhere],
        out_specs=vmem,
        scratch_shapes=scratch,
        compiler_params=pltpu.CompilerParams(
            collective_id=0, has_side_effects=True, vmem_limit_bytes=48 * 1024 * 1024
        ),
        name="spectral_layer",
    )(
        field, spectral_weight, local_weight, bias.reshape(1, channels),
        jnp.asarray(table_z), jnp.asarray(forward), jnp.asarray(back),
    )


def solution(mesh, ring=8, nx=4, nz=8):
    return jax.shard_map(
        functools.partial(on_device, ring, nx, nz),
        mesh=mesh,
        in_specs=(P(None, "gy", None, "gz"), P("gy", None, None, "gz", None), P(), P()),
        out_specs=P(None, "gy", None, "gz"),
        check_vma=False,
    )
```

time: 474 us -> 65.7 us (0.14)
  waiting for transfers between devices: 392 us -> 0 us
  Pallas kernels: 0 us -> 60.3 us
  blocking collectives: 24.3 us -> 0 us
  matrix products: 23.9 us -> 0 us
  between operations: 13.3 us -> 0.01 us
  local copies, waits for them, and re-layouts: 17.2 us -> 5.19 us
    reduce_scatter x2 -> x0, waiting for transfers between devices: 273 us -> none  [the longest x1 215 us: on_device(): lax.psum_scatter(jnp.concatenate([spec_real, spec_imag], -1).astype(jnp.b...]
    all_gather x2 -> x0, waiting for transfers between devices: 119 us -> none  [the longest x1 80.2 us: on_device(): piece = lax.all_gather(all_bands, 'gy', axis=0, tiled=True)]
    pallas_call x0 -> x1, Pallas kernels: none -> 60.3 us  [on_device(): pl.pallas_call(functools.partial(kernel, geometry, scale), out_shape=jax....]
    all_gather x1 -> x0, blocking collectives: 24.3 us -> none  [on_device(): all_bands = lax.all_gather(product, 'gz', axis=1, tiled=True)]
    dot_general x12 -> x0, matrix products: 23.9 us -> none  [the longest x1 3.54 us: on_device(): jnp.einsum('oc,xycz->xyoz', local_weight, field, preferred_element_type=j...]
    convert_element_type x2 -> x0, local copies, waits for them, and re-layouts: 8.24 us -> none  [on_device(): zmodes = lax.psum_scatter(partial_modes.reshape(lax.axis_size('gz') * ban...]
    slice x1 -> x0, local copies, waits for them, and re-layouts: 5.14 us -> none  [on_device(): prod_real = piece[..., :channels]]
  transfers between devices with their start and end apart: 4 -> 0, of which waited for: 4 -> 0; matrix products, arithmetic and copies ran while one was open for 3% -> 0% of each run, Pallas kernels for 0% -> 0%
where the time goes in v1:
time: 65.7 us; the launch traced here: 65.5 us
  Pallas kernels  60.3 us (92%)
  local copies, waits for them, and re-layouts  5.19 us (8%)
    pallas_call x1, Pallas kernels, on_device(): pl.pallas_call(functools.partial(kernel, geometry, scale), out_shape=jax....  60.3 us
    unnamed x9, local copies, waits for them, and re-layouts  5.19 us

profile of v1, /device:TPU:1, one launch (start us, length us, event | category | flops | bytes accessed | tf_op | source)
XLA Modules:
  0.0 65.5 jit_solution(11363877151052551615)
XLA Ops:
  0.0 0.0 copy-start
  0.0 1.6 %copy-done = bf16[8,16,64,128]{3,2,1,0:T(8,128)(2,1)S(1)} copy-done((bf16[8,16,64,128]{3,2,1,0:T(8,128)(2,1)S(1)}, bf16[8,16,64,128]{3,2,1,0:T(8,128)(2,1)}, u32[]{:S(2)}) %copy-start) | copy-done | bytes 2097176
  1.6 0.0 copy-start.1
  1.6 0.9 %copy-done.1 = bf16[2,32,2,4,64]{4,3,2,1,0:T(4,128)(2,1)S(1)} copy-done((bf16[2,32,2,4,64]{4,3,2,1,0:T(4,128)(2,1)S(1)}, bf16[2,32,2,4,64]{4,3,2,1,0:T(4,128)(2,1)}, u32[]{:S(2)}) %copy-start.1) | copy-done | bytes 65560
  2.5 0.0 copy-start.2
  2.5 0.7 %copy-done.2 = bf16[64,64]{1,0:T(8,128)(2,1)S(1)} copy-done((bf16[64,64]{1,0:T(8,128)(2,1)S(1)}, bf16[64,64]{1,0:T(8,128)(2,1)}, u32[]{:S(2)}) %copy-start.2) | copy-done | bytes 8216
  3.2 0.0 copy-start.3
  3.2 0.7 copy-done.3
  3.9 60.3 %spectral_layer.1 = bf16[8,16,64,128]{3,2,1,0:T(8,128)(2,1)S(1)} custom-call(bf16[8,16,64,128]{3,2,1,0:T(8,128)(2,1)S(1)} %copy-done, bf16[2,32,2,4,64]{4,3,2,1,0:T(4,128)(2,1)S(1)} %copy-done.1, bf16[64,64]{1,0:T(8,128)(2,1)S(1)} %copy-done.2, bf16[1,64]{1,0:T(2,128)(2,1)S(1)} %bitcast.1, f32[16,256,128]{2,1,0:T(8,128)} %constant.6.clone.table_z, ...), custom_call_target="tpu_custom_call" | custom-call | tf_op jit(solution)/shard_map/spectral_layer/pallas_call | solution.py:396
  64.1 1.3 %copy.9 = bf16[8,16,64,128]{3,2,1,0:T(8,128)(2,1)} copy(bf16[8,16,64,128]{3,2,1,0:T(8,128)(2,1)S(1)} %spectral_layer.1) | data formatting | bytes 4194304
Async XLA Ops:
  0.0 1.6 %copy-start = (bf16[8,16,64,128]{3,2,1,0:T(8,128)(2,1)S(1)}, bf16[8,16,64,128]{3,2,1,0:T(8,128)(2,1)}, u32[]{:S(2)}) copy-start(bf16[8,16,64,128]{3,2,1,0:T(8,128)(2,1)} %field.1) | copy-start | bytes 6291460
  1.6 0.9 %copy-start.1 = (bf16[2,32,2,4,64]{4,3,2,1,0:T(4,128)(2,1)S(1)}, bf16[2,32,2,4,64]{4,3,2,1,0:T(4,128)(2,1)}, u32[]{:S(2)}) copy-start(bf16[2,32,2,4,64]{4,3,2,1,0:T(4,128)(2,1)} %weight.1) | copy-start | bytes 196612
  2.5 0.7 %copy-start.2 = (bf16[64,64]{1,0:T(8,128)(2,1)S(1)}, bf16[64,64]{1,0:T(8,128)(2,1)}, u32[]{:S(2)}) copy-start(bf16[64,64]{1,0:T(8,128)(2,1)} %pointwise.1) | copy-start | bytes 24580
  3.2 0.7 %copy-start.3 = (bf16[64]{0:T(256)(128)(2,1)S(1)}, bf16[64]{0:T(256)(128)(2,1)}, u32[]{:S(2)}) copy-start(bf16[64]{0:T(256)(128)(2,1)} %param.10) | copy-start | bytes 388

commit v2 on v1

--- a/solution.py
+++ b/solution.py
@@ -14,6 +14,7 @@
 BF16 = jnp.bfloat16
 F32 = jnp.float32
 CHUNKS = 2
+VMEM_BYTES = 48 * 1024 * 1024
 
 
 def phase_of(number, modulus):
@@ -75,8 +76,8 @@
 
 def kernel(
     geometry, scale,
-    field, weight, pointwise, bias, table_z, table_f, table_b, out,
-    fv, wv, tz, tf, tb, acc, sib_out, sib_in, a_out, a_in, b_out, b_in, c_in, d_in,
+    field, weight, pointwise_in, bias_in, table_z, table_f, table_b, out,
+    fv, wv, pointwise, bias, tz, tf, tb, acc, sib_out, sib_in, a_out, a_in, b_out, b_in, c_in, d_in,
     w_mess, w_out, w_in, w_stage, w_full, small, wide, lin,
     local, local_f, local_w, sib_s, sib_r, a_s, a_r, b_s, b_r, c_s, c_r, d_s, d_r, e_s, e_r, w_s, w_r,
 ):
@@ -124,6 +125,10 @@
     for copy in get_f:
         copy.start()
     get_w.start()
+    get_mix = pltpu.make_async_copy(pointwise_in, pointwise, local.at[4])
+    get_bias = pltpu.make_async_copy(bias_in, bias, local.at[5])
+    get_mix.start()
+    get_bias.start()
     get_tf.start()
     get_tb.start()
 
@@ -134,7 +139,6 @@
         )
     for a, b in partners:
         pl.semaphore_signal(barrier, inc=1, device_id=plane(a, b), device_id_type=MESH)
-    pl.semaphore_wait(barrier, gz - 1 + gy - 1)
 
     get_tz.wait()
     member = lax.rem(lax.broadcasted_iota(jnp.int32, (gz * 16, depth), 0) // 4, 4)
@@ -142,36 +146,28 @@
         [jnp.where(member == i, tz[...], 0.0).astype(BF16) for i in range(4)], axis=1
     )
     own_rows = ring * 16
-    for ch in range(CHUNKS):
-        get_f[ch].wait()
-        for g in range(groups):
-            cells = jnp.concatenate(
-                [
-                    fv[ch * per : (ch + 1) * per, g * 4 + i].reshape(lanes, depth)
-                    for i in range(4)
-                ],
-                axis=1,
-            )
-            part = dot(table, cells, ((1,), (1,)))
-            sib_out[ch, g] = part[own_rows:].astype(BF16)
-            acc[ch, g] = part[:own_rows]
-            remote(
-                sib_out.at[ch, g], sib_in.at[ch, g], sib_s.at[ch, g], sib_r.at[ch, g], sibling
-            ).start()
-
-    for ch in range(CHUNKS):
-        for g in range(groups):
-            remote(
-                sib_out.at[ch, g], sib_in.at[ch, g], sib_s.at[ch, g], sib_r.at[ch, g], sibling
-            ).wait_recv()
-            total = acc[ch, g] + sib_in[ch, g].astype(F32)
-            acc[ch, g, 0:16] = total[0:16]
-            for t in range(1, ring):
-                a_out[ch, t - 1, g * 16 : (g + 1) * 16] = total[t * 16 : (t + 1) * 16].astype(BF16)
-        for t in range(1, ring):
-            remote(
-                a_out.at[ch, t - 1], a_in.at[ch, ring - 1 - t], a_s.at[ch], a_r.at[ch], chip(t)
-            ).start()
+
+    def cells(ch, g):
+        return jnp.concatenate(
+            [fv[ch * per : (ch + 1) * per, g * 4 + i].reshape(lanes, depth) for i in range(4)], axis=1
+        )
+
+    def to_sibling(ch, g):
+        return remote(
+            sib_out.at[ch, g], sib_in.at[ch, g], sib_s.at[ch, g], sib_r.at[ch, g], sibling
+        )
+
+    def z_sums(ch, g):
+        part = dot(table, cells(ch, g), ((1,), (1,)))
+        sib_out[ch, g] = part[own_rows:].astype(BF16)
+        acc[ch, g] = part[:own_rows]
+
+    get_f[0].wait()
+    for g in range(groups):
+        z_sums(0, g)
+    pl.semaphore_wait(barrier, gz - 1 + gy - 1)
+    for g in range(groups):
+        to_sibling(0, g).start()
 
     get_w.wait()
     for jj in range(2):
@@ -188,6 +184,33 @@
         dest = lax.rem(d + step, gz)
         remote(w_out.at[dest], w_in.at[d], w_s, w_r, {"gz": dest}).start()
 
+    for ch in range(1, CHUNKS):
+        get_f[ch].wait()
+        for g in range(groups):
+            z_sums(ch, g)
+            to_sibling(ch, g).start()
+
+    def towards(ch, t):
+        target, place = {
+            1: (1, 0), 7: (7, 1), 2: (2, 2), 6: (6, 3), 3: (1, 4), 5: (7, 5), 4: (6 if ch % 2 else 2, 6)
+        }[t]
+        return remote(
+            a_out.at[ch, t - 1], a_in.at[ch, place], a_s.at[ch], a_r.at[ch, place], chip(target)
+        )
+
+    for ch in range(CHUNKS):
+        for g in range(groups):
+            to_sibling(ch, g).wait_recv()
+            total = acc[ch, g] + sib_in[ch, g].astype(F32)
+            for t in (0, 2, 6):
+                acc[ch, g, t * 16 : (t + 1) * 16] = total[t * 16 : (t + 1) * 16]
+            for t in (3, 4, 5, 1, 7):
+                a_out[ch, t - 1, g * 16 : (g + 1) * 16] = total[t * 16 : (t + 1) * 16].astype(BF16)
+        for t in (3, 5, 4, 1, 7):
+            towards(ch, t).start()
+
+    get_mix.wait()
+    get_bias.wait()
     block = per * channels
     row_id = lax.broadcasted_iota(jnp.int32, (block, block), 0) // channels
     col_id = lax.broadcasted_iota(jnp.int32, (block, block), 1) // channels
@@ -199,25 +222,36 @@
         lax.rem(first, channels) == second, jnp.broadcast_to(bias[...].astype(F32), (block, channels)), 0.0
     ).astype(BF16)
     offset = dot(pick, jnp.ones((channels, 4 * depth), BF16))
+    def own_sums(ch, t):
+        return jnp.concatenate([acc[ch, g, t * 16 : (t + 1) * 16] for g in range(groups)], axis=0)
+
     for ch in range(CHUNKS):
         for g in range(groups):
-            cells = jnp.concatenate(
-                [
-                    fv[ch * per : (ch + 1) * per, g * 4 + i].reshape(lanes, depth)
-                    for i in range(4)
-                ],
-                axis=1,
-            )
-            lin[ch, g] = dot(mixing, cells) + offset
+            lin[ch, g] = dot(mixing, cells(ch, g)) + offset
+        towards(ch, 3).wait_recv()
+        towards(ch, 5).wait_recv()
+        towards(ch, 4).wait_recv()
+        across = a_in[ch, 6].astype(F32)
+        right = own_sums(ch, 2) + a_in[ch, 4].astype(F32)
+        left = own_sums(ch, 6) + a_in[ch, 5].astype(F32)
+        if ch % 2:
+            left = left + across
+        else:
+            right = right + across
+        a_out[ch, 1] = right.astype(BF16)
+        a_out[ch, 5] = left.astype(BF16)
+        towards(ch, 2).start()
+        towards(ch, 6).start()
 
     get_tf.wait()
     ahead = tf[...].astype(BF16)
     ahead = jnp.concatenate([ahead, ahead], axis=1)
     for ch in range(CHUNKS):
-        remote(a_in.at[ch], a_in.at[ch], a_s.at[ch], a_r.at[ch], chip(1)).wait_recv()
-        modes = jnp.concatenate([acc[ch, g, 0:16] for g in range(groups)], axis=0)
-        for t in range(ring - 1):
-            modes = modes + a_in[ch, t].astype(F32)
+        for t in (1, 7, 2, 6):
+            towards(ch, t).wait_recv()
+        modes = own_sums(ch, 0)
+        for place in range(4):
+            modes = modes + a_in[ch, place].astype(F32)
         high, low = split(modes)
         part = dot(ahead, jnp.concatenate([high, low], axis=0))
         part = part.reshape(gy, 8, lanes)
@@ -285,6 +319,14 @@
                 c_in.at[ch, 0], c_in.at[ch, slot(a, b)], c_s.at[ch], c_r.at[ch], plane(a, b)
             ).start()
 
+    def gather(ch, t, source=0):
+        return remote(
+            d_in.at[ch, 0, source], d_in.at[ch, 0, t], d_s.at[ch], d_r.at[ch, t], chip((source - t) % ring)
+        )
+
+    def share(ch, t):
+        return remote(d_in.at[ch, 0, t], d_in.at[ch, 1, t], e_s.at[ch, t], e_r.at[ch, t], sibling)
+
     get_tb.wait()
     behind = tb[...].astype(BF16)
     line = lax.broadcasted_iota(jnp.int32, (rows * 4, lanes), 0)
@@ -298,25 +340,30 @@
         bands = jnp.concatenate([bands[:, 0:8], bands[:, 8:16]], axis=2)
         bands = bands.reshape(gy * 8, lanes).astype(BF16)
         d_in[ch, 0, 0] = (dot(behind, bands) * factor).astype(BF16)
-        remote(d_in.at[ch, 0, 0], d_in.at[ch, 1, 0], e_s.at[ch, 0], e_r.at[ch, 0], sibling).start()
-        for t in range(1, ring):
-            remote(
-                d_in.at[ch, 0, 0], d_in.at[ch, 0, ring - t], d_s.at[ch], d_r.at[ch, ring - t], chip(t)
-            ).start()
-
-    order = sorted(range(1, ring), key=lambda t: min(t, ring - t))
-    for ch in range(CHUNKS):
-        for t in order:
-            remote(
-                d_in.at[ch, 0, 0], d_in.at[ch, 0, t], d_s.at[ch], d_r.at[ch, t], chip(1)
-            ).wait_recv()
-            remote(
-                d_in.at[ch, 0, t], d_in.at[ch, 1, t], e_s.at[ch, t], e_r.at[ch, t], sibling
-            ).start()
-        for t in [0] + order:
-            remote(
-                d_in.at[ch, 0, t], d_in.at[ch, 1, t], e_s.at[ch, t], e_r.at[ch, t], sibling
-            ).wait_recv()
+        for t in (6, 2, 7, 1):
+            gather(ch, t).start()
+        share(ch, 0).start()
+    for ch in range(CHUNKS):
+        gather(ch, 6).wait_recv()
+        gather(ch, 5, 6).start()
+        if ch % 2 == 0:
+            gather(ch, 4, 6).start()
+        gather(ch, 2).wait_recv()
+        gather(ch, 3, 2).start()
+        if ch % 2:
+            gather(ch, 4, 2).start()
+        share(ch, 6).start()
+        share(ch, 2).start()
+        for t in (7, 1):
+            gather(ch, t).wait_recv()
+            share(ch, t).start()
+
+    for ch in range(CHUNKS):
+        for t in (5, 3, 4):
+            gather(ch, t).wait_recv()
+            share(ch, t).start()
+        for t in range(ring):
+            share(ch, t).wait_recv()
         for g in range(groups):
             spectral = d_in[ch, :, :, g * 16 : (g + 1) * 16].reshape(gz * 16, lanes)
             value = gelu_tanh(dot(spectral, table, ((0,), (0,))) + lin[ch, g])
@@ -326,10 +373,8 @@
 
     for ch in range(CHUNKS):
         for g in range(groups):
-            remote(
-                sib_out.at[ch, g], sib_in.at[ch, g], sib_s.at[ch, g], sib_r.at[ch, g], sibling
-            ).wait_send()
-        remote(a_out.at[ch], a_in.at[ch], a_s.at[ch], a_r.at[ch], chip(1)).wait_send()
+            to_sibling(ch, g).wait_send()
+        remote(a_out.at[ch], a_in.at[ch], a_s.at[ch], a_r.at[ch, 0], chip(1)).wait_send()
         remote(
             b_out.at[ch, pl.ds(1, gy - 1)], b_in.at[ch, pl.ds(1, gy - 1)], b_s.at[ch], b_r.at[ch], plane(0, 1)
         ).wait_send()
@@ -340,9 +385,7 @@
             d_in.at[ch, 0, pl.ds(1, ring - 1)], d_in.at[ch, 0, pl.ds(1, ring - 1)], d_s.at[ch], d_r.at[ch, 1], chip(1)
         ).wait_send()
         for t in range(ring):
-            remote(
-                d_in.at[ch, 0, t], d_in.at[ch, 1, t], e_s.at[ch, t], e_r.at[ch, t], sibling
-            ).wait_send()
+            share(ch, t).wait_send()
     remote(w_in.at[pl.ds(0, gz - 1)], w_in.at[pl.ds(0, gz - 1)], w_s, w_r, chip(1)).wait_send()
 
 
@@ -362,6 +405,8 @@
     scratch = [
         pltpu.VMEM(field.shape, BF16),
         pltpu.VMEM(spectral_weight.shape, BF16),
+        pltpu.VMEM(local_weight.shape, BF16),
+        pltpu.VMEM((1, channels), BF16),
         pltpu.VMEM(table_z.shape[1:], F32),
         pltpu.VMEM(forward.shape[1:], F32),
         pltpu.VMEM(back.shape[1:], F32),
@@ -382,9 +427,9 @@
         pltpu.VMEM((half // 128, 16, 128), F32),
         pltpu.VMEM((per * 4, 2 * channels), F32),
         pltpu.VMEM((CHUNKS, groups, lanes, 4 * depth), F32),
-        dma((4,)), dma((CHUNKS,)), dma,
+        dma((6,)), dma((CHUNKS,)), dma,
         dma((CHUNKS, groups)), dma((CHUNKS, groups)),
-        dma((CHUNKS,)), dma((CHUNKS,)),
+        dma((CHUNKS,)), dma((CHUNKS, ring - 1)),
         dma((CHUNKS,)), dma((CHUNKS,)),
         dma((CHUNKS,)), dma((CHUNKS,)),
         dma((CHUNKS,)), dma((CHUNKS, ring)),
@@ -395,17 +440,22 @@
     vmem = pl.BlockSpec(memory_space=pltpu.VMEM)
     return pl.pallas_call(
         functools.partial(kernel, geometry, scale),
-        out_shape=jax.ShapeDtypeStruct(field.shape, BF16),
-        in_specs=[anywhere, anywhere, vmem, vmem, anywhere, anywhere, anywhere],
+        out_shape=pltpu.VMEM(field.shape, BF16),
+        in_specs=[anywhere] * 7,
         out_specs=vmem,
         scratch_shapes=scratch,
         compiler_params=pltpu.CompilerParams(
-            collective_id=0, has_side_effects=True, vmem_limit_bytes=48 * 1024 * 1024
+            collective_id=0, has_side_effects=True, vmem_limit_bytes=VMEM_BYTES
         ),
         name="spectral_layer",
     )(
-        field, spectral_weight, local_weight, bias.reshape(1, channels),
-        jnp.asarray(table_z), jnp.asarray(forward), jnp.asarray(back),
+        *[
+            pltpu.with_memory_space_constraint(array, pltpu.HBM)
+            for array in (
+                field, spectral_weight, local_weight, bias.reshape(1, channels),
+                jnp.asarray(table_z), jnp.asarray(forward), jnp.asarray(back),
+            )
+        ]
     )
 
 

time: 65.7 us -> 58 us (0.88)
  local copies, waits for them, and re-layouts: 5.19 us -> 1.32 us
  Pallas kernels: 60.3 us -> 56.5 us
    unnamed x9 -> x1, local copies, waits for them, and re-layouts: 5.19 us -> 1.32 us
    pallas_call x1, Pallas kernels: 60.3 us -> 56.5 us  [on_device(): pl.pallas_call(functools.partial(kernel, geometry, scale), out_shape=pltp...]
where the time goes in v2:
time: 58 us; the launch traced here: 57.9 us
  Pallas kernels  56.5 us (97%)
  local copies, waits for them, and re-layouts  1.32 us (2%)
    pallas_call x1, Pallas kernels, on_device(): pl.pallas_call(functools.partial(kernel, geometry, scale), out_shape=pltp...  56.5 us
    unnamed x1, local copies, waits for them, and re-layouts  1.32 us

profile of v2, /device:TPU:1, one launch (start us, length us, event | category | flops | bytes accessed | tf_op | source)
XLA Modules:
  0.0 57.9 jit_solution(2536729366923080269)
XLA Ops:
  0.0 56.5 %spectral_layer.1 = bf16[8,16,64,128]{3,2,1,0:T(8,128)(2,1)S(1)} custom-call(bf16[8,16,64,128]{3,2,1,0:T(8,128)(2,1)} %field.1, bf16[2,32,2,4,64]{4,3,2,1,0:T(4,128)(2,1)} %weight.1, bf16[64,64]{1,0:T(8,128)(2,1)} %pointwise_in.1, bf16[1,64]{1,0:T(2,128)(2,1)} %bitcast.1, f32[16,256,128]{2,1,0:T(8,128)} %constant.6.clone.table_z, ...), custom_call_target="tpu_custom_call" | custom-call | tf_op jit(solution)/shard_map/spectral_layer/pallas_call | solution.py:441
  56.5 1.3 %copy.9 = bf16[8,16,64,128]{3,2,1,0:T(8,128)(2,1)} copy(bf16[8,16,64,128]{3,2,1,0:T(8,128)(2,1)S(1)} %spectral_layer.1) | data formatting | bytes 4194304

commit v3 on v2

v3 whole, which is shorter than its diff:
```python
import functools
import math

import jax
import jax.numpy as jnp
import ml_dtypes
import numpy as np
from jax import lax
from jax.experimental import pallas as pl
from jax.experimental.pallas import tpu as pltpu
from jax.sharding import PartitionSpec as P

MESH = pl.DeviceIdType.MESH
BF16 = jnp.bfloat16
F32 = jnp.float32
CHUNKS = 4
ORDER = [
    [("y", 0), ("y", 1), ("y", 2), ("y", 3), ("p", 0), ("p", 1), ("p", 2), ("p", 3)],
    [("l", 0), ("l", 1), ("z", 0), ("l", 2), ("z", 1), ("l", 3), ("z", 2), ("z", 3)],
]
VMEM_BYTES = 48 * 1024 * 1024


def phase_of(number, modulus):
    return (number % modulus).astype(np.float32) * np.float32(2.0 * math.pi / modulus)


def rounded(array):
    return np.asarray(array, np.float32).astype(ml_dtypes.bfloat16).astype(np.float32)


def z_tables(ring, depth):
    size = 2 * ring
    cell = np.arange(depth)
    tables = []
    for d in range(size):
        owner = np.array(
            [((d // 2 + t) % ring) * 2 + (d % 2 ^ r) for r in range(2) for t in range(ring)]
        )
        mode = owner[:, None] * 2 + np.arange(2)
        angle = phase_of(mode[:, :, None] * (cell * size + d), depth * size)
        base = np.stack([np.cos(angle), -np.sin(angle)], 2)
        tables.append(np.repeat(base[:, None], 4, 1).reshape(size * 16, depth))
    return rounded(np.stack(tables))


def y_tables(nx, nz, rows):
    size = nx * nz
    total = rows * size
    forward, back = [], []
    for e in range(size):
        owner = np.array(
            [((e // nz + a) % nx) * nz + (e % nz + b) % nz for a in range(nx) for b in range(nz)]
        )
        mode = owner[:, None] * 2 + np.arange(2)
        wave = np.where(mode < size, mode, mode + total - 2 * size)
        angle = phase_of(wave[:, :, None] * (np.arange(rows) * size + e), total)
        cosine, sine = np.cos(angle), np.sin(angle)
        there = np.stack([np.stack([cosine, sine], -1), np.stack([-sine, cosine], -1)], 2)
        there = np.einsum("ujqyp,kl->ujkqylp", there, np.eye(2))
        forward.append(there.reshape(size * 8, rows * 4))
        here = np.stack([np.stack([cosine, -sine], -1), np.stack([sine, cosine], -1)], 2)
        here = np.einsum("ujqyp,kl->ykqujlp", here, np.eye(2))
        back.append(here.reshape(rows * 4, size * 8))
    return rounded(np.stack(forward)), rounded(np.stack(back))


def gelu_tanh(value):
    return 0.5 * value * (1.0 + jnp.tanh(0.7978845608 * (value + 0.044715 * value * value * value)))


def split(value):
    high = value.astype(BF16)
    return high, (value - high.astype(F32)).astype(BF16)


def dot(left, right, dims=((1,), (0,))):
    return lax.dot_general(left, right, (dims, ((), ())), preferred_element_type=F32)


def kernel(
    geometry, scale,
    field, weight, pointwise_in, bias_in, table_z, table_f, table_b, out,
    fv, wv, pointwise, bias, tz, tf, tb, acc, sib_out, sib_in, a_out, a_in, b_out, b_in, c_in, d_in,
    w_mess, w_out, w_in, w_stage, w_full, small, wide, lin,
    local, local_f, local_w, sib_s, sib_r, a_s, a_r, b_s, b_r, c_s, c_r, d_s, d_r, e_s, e_r, w_s, w_r,
):
    ring, nx, nz, planes, rows, channels, depth = geometry
    gz, gy = 2 * ring, nx * nz
    chunks = range(CHUNKS)
    per = planes // CHUNKS
    lanes = per * channels
    fold = lanes // (2 * channels)
    groups = rows // 4
    band = channels // gz
    d = lax.axis_index("gz")
    e = lax.axis_index("gy")
    core = lax.rem(d, 2)

    def chip(t):
        return {"gz": lax.rem(d + 2 * t, gz)}

    sibling = {"gz": d + 1 - 2 * core}
    ex, ez = e // nz, lax.rem(e, nz)

    def plane(a, b):
        return {"gy": lax.rem(ex + a, nx) * nz + lax.rem(ez + b, nz)}

    partners = sorted(
        [(a, b) for a in range(nx) for b in range(nz)][1:],
        key=lambda step: -min(step[0], nx - step[0]) - min(step[1], nz - step[1]),
    )

    def slot(a, b):
        return ((nx - a) % nx) * nz + (nz - b) % nz

    def remote(src, dst, send, recv, device):
        return pltpu.make_async_remote_copy(
            src_ref=src, dst_ref=dst, send_sem=send, recv_sem=recv, device_id=device, device_id_type=MESH
        )

    def to_sibling(ch):
        return remote(sib_out.at[ch], sib_in.at[ch], sib_s.at[ch], sib_r.at[ch], sibling)

    def towards(ch, t):
        target, place = {
            1: (1, 0), 7: (7, 1), 2: (2, 2), 6: (6, 3), 3: (1, 4), 5: (7, 5), 4: (6 if ch % 2 else 2, 6)
        }[t]
        return remote(
            a_out.at[ch, t - 1], a_in.at[ch, place], a_s.at[ch], a_r.at[ch, place], chip(target)
        )

    def weights_to(step):
        dest = lax.rem(d + step, gz)
        return remote(w_out.at[dest], w_in.at[d], w_s, w_r, {"gz": dest})

    def spread(ch, a, b):
        return remote(
            b_out.at[ch, a * nz + b], b_in.at[ch, slot(a, b)], b_s.at[ch], b_r.at[ch], plane(a, b)
        )

    def all_spread(ch):
        rest = pl.ds(1, gy - 1)
        return remote(b_out.at[ch, rest], b_in.at[ch, rest], b_s.at[ch], b_r.at[ch], plane(0, 1))

    def join(ch, a, b):
        return remote(c_in.at[ch, 0], c_in.at[ch, slot(a, b)], c_s.at[ch], c_r.at[ch], plane(a, b))

    def all_join(ch):
        rest = pl.ds(1, gy - 1)
        return remote(c_in.at[ch, rest], c_in.at[ch, rest], c_s.at[ch], c_r.at[ch], plane(0, 1))

    def gather(ch, t, source=0):
        return remote(
            d_in.at[ch, 0, source], d_in.at[ch, 0, t], d_s.at[ch], d_r.at[ch, t], chip((source - t) % ring)
        )

    def share(ch, t):
        return remote(d_in.at[ch, 0, t], d_in.at[ch, 1, t], e_s.at[ch, t], e_r.at[ch, t], sibling)

    get_tz = pltpu.make_async_copy(table_z.at[d], tz, local.at[0])
    get_f = [
        pltpu.make_async_copy(
            field.at[pl.ds(ch * per, per)], fv.at[pl.ds(ch * per, per)], local_f.at[ch]
        )
        for ch in chunks
    ]
    get_w = pltpu.make_async_copy(weight, wv, local.at[1])
    get_tf = pltpu.make_async_copy(table_f.at[e], tf, local.at[2])
    get_tb = pltpu.make_async_copy(table_b.at[e], tb, local.at[3])
    get_mix = pltpu.make_async_copy(pointwise_in, pointwise, local.at[4])
    get_bias = pltpu.make_async_copy(bias_in, bias, local.at[5])
    get_tz.start()
    for copy in get_f:
        copy.start()
    for copy in (get_w, get_tf, get_tb, get_mix, get_bias):
        copy.start()

    barrier = pltpu.get_barrier_semaphore()
    for step in range(1, gz):
        pl.semaphore_signal(
            barrier, inc=1, device_id={"gz": lax.rem(d + step, gz)}, device_id_type=MESH
        )
    for a, b in partners:
        pl.semaphore_signal(barrier, inc=1, device_id=plane(a, b), device_id_type=MESH)

    get_tz.wait()
    member = lax.rem(lax.broadcasted_iota(jnp.int32, (gz * 16, depth), 0) // 4, 4)
    table = jnp.concatenate(
        [jnp.where(member == i, tz[...], 0.0).astype(BF16) for i in range(4)], axis=1
    )
    own_rows = ring * 16

    def cells(ch, g):
        return jnp.concatenate(
            [fv[ch * per : (ch + 1) * per, g * 4 + i].reshape(lanes, depth) for i in range(4)], axis=1
        )

    for ch in chunks:
        get_f[ch].wait()
        for g in range(groups):
            part = dot(table, cells(ch, g), ((1,), (1,)))
            sib_out[ch, g] = part[own_rows:].astype(BF16)
            acc[ch, g] = part[:own_rows]

    get_w.wait()
    for jj in range(2):
        for k in range(2 * gz):
            for p in range(2):
                row = (jj * 2 + k % 2) * band
                w_mess[k // 2, row : row + band, p * channels : (p + 1) * channels] = wv[
                    jj, k, p
                ].astype(F32)
    w_out[...] = w_mess[...].astype(BF16)
    own_w = pltpu.make_async_copy(w_out.at[d], w_in.at[d], local_w)
    own_w.start()

    pl.semaphore_wait(barrier, gz - 1 + gy - 1)
    for ch in chunks:
        to_sibling(ch).start()
    for step in range(1, gz):
        weights_to(step).start()

    for ch in chunks:
        to_sibling(ch).wait_recv()
        for g in range(groups):
            total = acc[ch, g] + sib_in[ch, g].astype(F32)
            for t in (0, 2, 6):
                acc[ch, g, t * 16 : (t + 1) * 16] = total[t * 16 : (t + 1) * 16]
            for t in (3, 4, 5, 1, 7):
                a_out[ch, t - 1, g * 16 : (g + 1) * 16] = total[t * 16 : (t + 1) * 16].astype(BF16)
        for t in (4, 3, 5):
            towards(ch, t).start()
    for ch in chunks:
        for t in (1, 7):
            towards(ch, t).start()

    get_mix.wait()
    get_bias.wait()
    row_id = lax.broadcasted_iota(jnp.int32, (lanes, lanes), 0) // channels
    col_id = lax.broadcasted_iota(jnp.int32, (lanes, lanes), 1) // channels
    row = jnp.concatenate([pointwise[...].astype(F32)] * per, axis=1)
    mixing = jnp.where(row_id == col_id, jnp.concatenate([row] * per, axis=0), 0.0).astype(BF16)
    first = lax.broadcasted_iota(jnp.int32, (lanes, channels), 0)
    second = lax.broadcasted_iota(jnp.int32, (lanes, channels), 1)
    pick = jnp.where(
        lax.rem(first, channels) == second, jnp.broadcast_to(bias[...].astype(F32), (lanes, channels)), 0.0
    ).astype(BF16)
    offset = dot(pick, jnp.ones((channels, 4 * depth), BF16))
    for ch in chunks:
        for g in range(groups):
            lin[ch, g] = dot(mixing, cells(ch, g)) + offset

    def own_sums(ch, t):
        return jnp.concatenate([acc[ch, g, t * 16 : (t + 1) * 16] for g in range(groups)], axis=0)

    for ch in chunks:
        for t in (3, 5, 4):
            towards(ch, t).wait_recv()
        across = a_in[ch, 6].astype(F32)
        right = own_sums(ch, 2) + a_in[ch, 4].astype(F32)
        left = own_sums(ch, 6) + a_in[ch, 5].astype(F32)
        if ch % 2:
            left = left + across
        else:
            right = right + across
        a_out[ch, 1] = right.astype(BF16)
        a_out[ch, 5] = left.astype(BF16)
        towards(ch, 2).start()
        towards(ch, 6).start()

    get_tf.wait()
    ahead = tf[...].astype(BF16)
    ahead = jnp.concatenate([ahead, ahead], axis=1)
    for ch in chunks:
        for t in (1, 7, 2, 6):
            towards(ch, t).wait_recv()
        modes = own_sums(ch, 0)
        for place in range(4):
            modes = modes + a_in[ch, place].astype(F32)
        high, low = split(modes)
        part = dot(ahead, jnp.concatenate([high, low], axis=0)).reshape(gy, 8, lanes)
        part = jnp.concatenate([part[:, :, h * 128 : (h + 1) * 128] for h in range(fold)], axis=1)
        b_out[ch] = part.astype(BF16)
        b_in[ch, 0] = b_out[ch, 0]
        for a, b in partners:
            spread(ch, a, b).start()

    own_w.wait()
    rest = pl.ds(0, gz - 1)
    remote(w_in.at[rest], w_in.at[rest], w_s, w_r, chip(1)).wait_recv()
    w_mess[...] = w_in[...].astype(F32)
    for source in range(gz):
        for jk in range(4):
            w_stage[jk, source * band : (source + 1) * band] = w_mess[
                source, jk * band : (jk + 1) * band
            ]
    sign = jnp.where(
        lax.broadcasted_iota(jnp.int32, (channels, 2 * channels), 1) < channels, -1.0, 1.0
    )
    for jk in range(4):
        upper = w_stage[jk]
        lower = pltpu.roll(upper, channels, 1) * sign
        w_full[jk] = jnp.concatenate([upper, lower], axis=0).astype(BF16)

    pairs = fold * 4
    for ch in chunks:
        all_spread(ch).wait_recv()
        small[...] = jnp.sum(b_in[ch].astype(F32), axis=0)
        real = small[pl.ds(0, pairs, stride=2), :]
        imag = small[pl.ds(1, pairs, stride=2), :]
        for x in range(2):
            part = slice(x * channels, (x + 1) * channels)
            wide[x * pairs : (x + 1) * pairs, :] = jnp.concatenate([real[:, part], imag[:, part]], axis=1)
        products = []
        for jk in range(4):
            high, low = split(wide[pl.ds(jk, per, stride=4), :])
            both = dot(jnp.concatenate([high.astype(F32), low.astype(F32)], axis=0).astype(BF16), w_full[jk])
            products.append(both[:per] + both[per:])
        for jk in range(4):
            wide[pl.ds(jk, per, stride=4), :] = products[jk]
        pieces = [wide[x * pairs : (x + 1) * pairs, :] for x in range(2)]
        small[pl.ds(0, pairs, stride=2), :] = jnp.concatenate(
            [piece[:, :channels] for piece in pieces], axis=1
        )
        small[pl.ds(1, pairs, stride=2), :] = jnp.concatenate(
            [piece[:, channels:] for piece in pieces], axis=1
        )
        c_in[ch, 0] = small[...].astype(BF16)
        for a, b in partners:
            join(ch, a, b).start()

    get_tb.wait()
    behind = tb[...].astype(BF16)
    line = lax.broadcasted_iota(jnp.int32, (rows * 4, lanes), 0)
    low_mode = jnp.logical_and(lax.rem(line, 4) < 2, d == 0)
    factor = jnp.where(low_mode, scale, 2.0 * scale)

    def back_y(ch):
        all_join(ch).wait_recv()
        bands = c_in[ch].astype(F32)
        bands = jnp.concatenate([bands[:, h * 8 : (h + 1) * 8] for h in range(fold)], axis=2)
        bands = bands.reshape(gy * 8, lanes).astype(BF16)
        d_in[ch, 0, 0] = (dot(behind, bands) * factor).astype(BF16)
        for t in (6, 2):
            gather(ch, t).start()
        share(ch, 0).start()

    def pass_on(ch):
        for t, following in ((6, 5), (2, 3)):
            gather(ch, t).wait_recv()
            gather(ch, following, t).start()
            if t == (2 if ch % 2 else 6):
                gather(ch, 4, t).start()
            share(ch, t).start()
        for t in (7, 1):
            gather(ch, t).start()

    def last_bands(ch):
        for t in (7, 1, 5, 3, 4):
            gather(ch, t).wait_recv()
            share(ch, t).start()

    def back_z(ch):
        for t in range(ring):
            share(ch, t).wait_recv()
        for g in range(groups):
            spectral = d_in[ch, :, :, g * 16 : (g + 1) * 16].reshape(gz * 16, lanes)
            value = gelu_tanh(dot(spectral, table, ((0,), (0,))) + lin[ch, g])
            value = value.astype(BF16).reshape(per, channels, 4 * depth)
            for i in range(4):
                out[ch * per : (ch + 1) * per, g * 4 + i] = value[:, :, i * depth : (i + 1) * depth]

    for step in ORDER:
        for name, ch in step:
            {"y": back_y, "p": pass_on, "l": last_bands, "z": back_z}[name](ch)

    for ch in chunks:
        to_sibling(ch).wait_send()
        remote(a_out.at[ch], a_in.at[ch], a_s.at[ch], a_r.at[ch, 0], chip(1)).wait_send()
        all_spread(ch).wait_send()
        all_join(ch).wait_send()
        others = pl.ds(1, ring - 1)
        remote(
            d_in.at[ch, 0, others], d_in.at[ch, 0, others], d_s.at[ch], d_r.at[ch, 1], chip(1)
        ).wait_send()
        for t in range(ring):
            share(ch, t).wait_send()
    remote(w_in.at[rest], w_in.at[rest], w_s, w_r, chip(1)).wait_send()


def on_device(ring, nx, nz, field, spectral_weight, local_weight, bias):
    planes, rows, channels, depth = field.shape
    gz, gy = 2 * ring, nx * nz
    geometry = (ring, nx, nz, planes, rows, channels, depth)
    scale = 1.0 / (rows * gy * depth * gz)
    forward, back = y_tables(nx, nz, rows)
    table_z = z_tables(ring, depth)
    per = planes // CHUNKS
    lanes = per * channels
    fold = lanes // (2 * channels)
    groups = rows // 4
    band = channels // gz
    dma = pltpu.SemaphoreType.DMA
    scratch = [
        pltpu.VMEM(field.shape, BF16),
        pltpu.VMEM(spectral_weight.shape, BF16),
        pltpu.VMEM(local_weight.shape, BF16),
        pltpu.VMEM((1, channels), BF16),
        pltpu.VMEM(table_z.shape[1:], F32),
        pltpu.VMEM(forward.shape[1:], F32),
        pltpu.VMEM(back.shape[1:], F32),
        pltpu.VMEM((CHUNKS, groups, ring * 16, lanes), F32),
        pltpu.VMEM((CHUNKS, groups, ring * 16, lanes), BF16),
        pltpu.VMEM((CHUNKS, groups, ring * 16, lanes), BF16),
        pltpu.VMEM((CHUNKS, ring - 1, rows * 4, lanes), BF16),
        pltpu.VMEM((CHUNKS, ring - 1, rows * 4, lanes), BF16),
        pltpu.VMEM((CHUNKS, gy, 8 * fold, 2 * channels), BF16),
        pltpu.VMEM((CHUNKS, gy, 8 * fold, 2 * channels), BF16),
        pltpu.VMEM((CHUNKS, gy, 8 * fold, 2 * channels), BF16),
        pltpu.VMEM((CHUNKS, 2, ring, rows * 4, lanes), BF16),
        pltpu.VMEM((gz, 4 * band, 2 * channels), F32),
        pltpu.VMEM((gz, 4 * band, 2 * channels), BF16),
        pltpu.VMEM((gz, 4 * band, 2 * channels), BF16),
        pltpu.VMEM((4, channels, 2 * channels), F32),
        pltpu.VMEM((4, 2 * channels, 2 * channels), BF16),
        pltpu.VMEM((8 * fold, 2 * channels), F32),
        pltpu.VMEM((per * 4, 2 * channels), F32),
        pltpu.VMEM((CHUNKS, groups, lanes, 4 * depth), F32),
        dma((6,)), dma((CHUNKS,)), dma,
        dma((CHUNKS,)), dma((CHUNKS,)),
        dma((CHUNKS,)), dma((CHUNKS, ring - 1)),
        dma((CHUNKS,)), dma((CHUNKS,)),
        dma((CHUNKS,)), dma((CHUNKS,)),
        dma((CHUNKS,)), dma((CHUNKS, ring)),
        dma((CHUNKS, ring)), dma((CHUNKS, ring)),
        dma, dma,
    ]
    anywhere = pl.BlockSpec(memory_space=pltpu.HBM)
    vmem = pl.BlockSpec(memory_space=pltpu.VMEM)
    return pl.pallas_call(
        functools.partial(kernel, geometry, scale),
        out_shape=pltpu.VMEM(field.shape, BF16),
        in_specs=[anywhere] * 7,
        out_specs=vmem,
        scratch_shapes=scratch,
        compiler_params=pltpu.CompilerParams(
            collective_id=0, has_side_effects=True, vmem_limit_bytes=VMEM_BYTES
        ),
        name="spectral_layer",
    )(
        *[
            pltpu.with_memory_space_constraint(array, pltpu.HBM)
            for array in (
                field, spectral_weight, local_weight, bias.reshape(1, channels),
                jnp.asarray(table_z), jnp.asarray(forward), jnp.asarray(back),
            )
        ]
    )


def solution(mesh, ring=8, nx=4, nz=8):
    return jax.shard_map(
        functools.partial(on_device, ring, nx, nz),
        mesh=mesh,
        in_specs=(P(None, "gy", None, "gz"), P("gy", None, None, "gz", None), P(), P()),
        out_specs=P(None, "gy", None, "gz"),
        check_vma=False,
    )
```

time: 58 us -> 54.4 us (0.938)
  Pallas kernels: 56.5 us -> 52.9 us
    pallas_call x1, Pallas kernels: 56.5 us -> 52.9 us  [on_device(): pl.pallas_call(functools.partial(kernel, geometry, scale), out_shape=pltp...]
where the time goes in v3:
time: 54.4 us; the launch traced here: 54.2 us
  Pallas kernels  52.9 us (97%)
  local copies, waits for them, and re-layouts  1.32 us (2%)
    pallas_call x1, Pallas kernels, on_device(): pl.pallas_call(functools.partial(kernel, geometry, scale), out_shape=pltp...  52.9 us
    unnamed x1, local copies, waits for them, and re-layouts  1.32 us

profile of v3, /device:TPU:1, one launch (start us, length us, event | category | flops | bytes accessed | tf_op | source)
XLA Modules:
  0.0 54.2 jit_solution(6894811334845653206)
XLA Ops:
  0.0 52.9 %spectral_layer.1 = bf16[8,16,64,128]{3,2,1,0:T(8,128)(2,1)S(1)} custom-call(bf16[8,16,64,128]{3,2,1,0:T(8,128)(2,1)} %field.1, bf16[2,32,2,4,64]{4,3,2,1,0:T(4,128)(2,1)} %weight.1, bf16[64,64]{1,0:T(8,128)(2,1)} %pointwise_in.1, bf16[1,64]{1,0:T(2,128)(2,1)} %bitcast.1, f32[16,256,128]{2,1,0:T(8,128)} %constant.6.clone.table_z, ...), custom_call_target="tpu_custom_call" | custom-call | tf_op jit(solution)/shard_map/spectral_layer/pallas_call | solution.py:441
  52.9 1.3 %copy.9 = bf16[8,16,64,128]{3,2,1,0:T(8,128)(2,1)} copy(bf16[8,16,64,128]{3,2,1,0:T(8,128)(2,1)S(1)} %spectral_layer.1) | data formatting | bytes 4194304

commit v4 on v3

--- a/solution.py
+++ b/solution.py
@@ -66,7 +66,9 @@
 
 
 def gelu_tanh(value):
-    return 0.5 * value * (1.0 + jnp.tanh(0.7978845608 * (value + 0.044715 * value * value * value)))
+    half = 0.5 * value
+    inner = value * (0.7978845608 + (0.7978845608 * 0.044715) * (value * value))
+    return half + half * jnp.tanh(inner)
 
 
 def split(value):
@@ -158,6 +160,14 @@
     def share(ch, t):
         return remote(d_in.at[ch, 0, t], d_in.at[ch, 1, t], e_s.at[ch, t], e_r.at[ch, t], sibling)
 
+    barrier = pltpu.get_barrier_semaphore()
+    for a, b in partners:
+        pl.semaphore_signal(barrier, inc=1, device_id=plane(a, b), device_id_type=MESH)
+    for step in range(1, gz):
+        pl.semaphore_signal(
+            barrier, inc=1, device_id={"gz": lax.rem(d + step, gz)}, device_id_type=MESH
+        )
+
     get_tz = pltpu.make_async_copy(table_z.at[d], tz, local.at[0])
     get_f = [
         pltpu.make_async_copy(
@@ -176,14 +186,6 @@
     for copy in (get_w, get_tf, get_tb, get_mix, get_bias):
         copy.start()
 
-    barrier = pltpu.get_barrier_semaphore()
-    for step in range(1, gz):
-        pl.semaphore_signal(
-            barrier, inc=1, device_id={"gz": lax.rem(d + step, gz)}, device_id_type=MESH
-        )
-    for a, b in partners:
-        pl.semaphore_signal(barrier, inc=1, device_id=plane(a, b), device_id_type=MESH)
-
     get_tz.wait()
     member = lax.rem(lax.broadcasted_iota(jnp.int32, (gz * 16, depth), 0) // 4, 4)
     table = jnp.concatenate(
@@ -193,15 +195,18 @@
 
     def cells(ch, g):
         return jnp.concatenate(
-            [fv[ch * per : (ch + 1) * per, g * 4 + i].reshape(lanes, depth) for i in range(4)], axis=1
-        )
-
-    for ch in chunks:
+            [fv[ch * per : (ch + 2) * per, g * 4 + i].reshape(2 * lanes, depth) for i in range(4)], axis=1
+        )
+
+    for ch in chunks[::2]:
         get_f[ch].wait()
+        get_f[ch + 1].wait()
         for g in range(groups):
             part = dot(table, cells(ch, g), ((1,), (1,)))
-            sib_out[ch, g] = part[own_rows:].astype(BF16)
-            acc[ch, g] = part[:own_rows]
+            for side in range(2):
+                mine = part[:, side * lanes : (side + 1) * lanes]
+                sib_out[ch + side, g] = mine[own_rows:].astype(BF16)
+                acc[ch + side, g] = mine[:own_rows]
 
     get_w.wait()
     for jj in range(2):
@@ -237,19 +242,21 @@
 
     get_mix.wait()
     get_bias.wait()
-    row_id = lax.broadcasted_iota(jnp.int32, (lanes, lanes), 0) // channels
-    col_id = lax.broadcasted_iota(jnp.int32, (lanes, lanes), 1) // channels
-    row = jnp.concatenate([pointwise[...].astype(F32)] * per, axis=1)
-    mixing = jnp.where(row_id == col_id, jnp.concatenate([row] * per, axis=0), 0.0).astype(BF16)
-    first = lax.broadcasted_iota(jnp.int32, (lanes, channels), 0)
-    second = lax.broadcasted_iota(jnp.int32, (lanes, channels), 1)
+    row_id = lax.broadcasted_iota(jnp.int32, (2 * lanes, 2 * lanes), 0) // channels
+    col_id = lax.broadcasted_iota(jnp.int32, (2 * lanes, 2 * lanes), 1) // channels
+    row = jnp.concatenate([pointwise[...].astype(F32)] * (2 * per), axis=1)
+    mixing = jnp.where(row_id == col_id, jnp.concatenate([row] * (2 * per), axis=0), 0.0).astype(BF16)
+    first = lax.broadcasted_iota(jnp.int32, (2 * lanes, channels), 0)
+    second = lax.broadcasted_iota(jnp.int32, (2 * lanes, channels), 1)
     pick = jnp.where(
-        lax.rem(first, channels) == second, jnp.broadcast_to(bias[...].astype(F32), (lanes, channels)), 0.0
+        lax.rem(first, channels) == second, jnp.broadcast_to(bias[...].astype(F32), (2 * lanes, channels)), 0.0
     ).astype(BF16)
     offset = dot(pick, jnp.ones((channels, 4 * depth), BF16))
-    for ch in chunks:
+    for ch in chunks[::2]:
         for g in range(groups):
-            lin[ch, g] = dot(mixing, cells(ch, g)) + offset
+            mapped = dot(mixing, cells(ch, g)) + offset
+            lin[ch, g] = mapped[:lanes]
+            lin[ch + 1, g] = mapped[lanes:]
 
     def own_sums(ch, t):
         return jnp.concatenate([acc[ch, g, t * 16 : (t + 1) * 16] for g in range(groups)], axis=0)

time: 54.4 us -> 54.2 us (level)
  no operation moved by 1% of the time
where the time goes in v4:
time: 54.2 us; the launch traced here: 54 us
  Pallas kernels  52.7 us (97%)
  local copies, waits for them, and re-layouts  1.32 us (2%)
    pallas_call x1, Pallas kernels, on_device(): pl.pallas_call(functools.partial(kernel, geometry, scale), out_shape=pltp...  52.7 us
    unnamed x1, local copies, waits for them, and re-layouts  1.32 us

profile of v4, /device:TPU:1, one launch (start us, length us, event | category | flops | bytes accessed | tf_op | source)
XLA Modules:
  0.0 54.0 jit_solution(2404731837285172580)
XLA Ops:
  0.0 52.7 %spectral_layer.1 = bf16[8,16,64,128]{3,2,1,0:T(8,128)(2,1)S(1)} custom-call(bf16[8,16,64,128]{3,2,1,0:T(8,128)(2,1)} %field.1, bf16[2,32,2,4,64]{4,3,2,1,0:T(4,128)(2,1)} %weight.1, bf16[64,64]{1,0:T(8,128)(2,1)} %pointwise_in.1, bf16[1,64]{1,0:T(2,128)(2,1)} %bitcast.1, f32[16,256,128]{2,1,0:T(8,128)} %constant.6.clone.table_z, ...), custom_call_target="tpu_custom_call" | custom-call | tf_op jit(solution)/shard_map/spectral_layer/pallas_call | solution.py:448
  52.7 1.3 %copy.9 = bf16[8,16,64,128]{3,2,1,0:T(8,128)(2,1)} copy(bf16[8,16,64,128]{3,2,1,0:T(8,128)(2,1)S(1)} %spectral_layer.1) | data formatting | bytes 4194304

commit v5 on v4

--- a/solution.py
+++ b/solution.py
@@ -157,8 +157,11 @@
             d_in.at[ch, 0, source], d_in.at[ch, 0, t], d_s.at[ch], d_r.at[ch, t], chip((source - t) % ring)
         )
 
-    def share(ch, t):
-        return remote(d_in.at[ch, 0, t], d_in.at[ch, 1, t], e_s.at[ch, t], e_r.at[ch, t], sibling)
+    def share(ch, part):
+        bands = (pl.ds(0, 3), pl.ds(6, 2), pl.ds(3, 3))[part]
+        return remote(
+            d_in.at[ch, 0, bands], d_in.at[ch, 1, bands], e_s.at[ch, part], e_r.at[ch, part], sibling
+        )
 
     barrier = pltpu.get_barrier_semaphore()
     for a, b in partners:
@@ -349,9 +352,8 @@
         bands = jnp.concatenate([bands[:, h * 8 : (h + 1) * 8] for h in range(fold)], axis=2)
         bands = bands.reshape(gy * 8, lanes).astype(BF16)
         d_in[ch, 0, 0] = (dot(behind, bands) * factor).astype(BF16)
-        for t in (6, 2):
+        for t in (6, 2, 7, 1):
             gather(ch, t).start()
-        share(ch, 0).start()
 
     def pass_on(ch):
         for t, following in ((6, 5), (2, 3)):
@@ -359,18 +361,18 @@
             gather(ch, following, t).start()
             if t == (2 if ch % 2 else 6):
                 gather(ch, 4, t).start()
-            share(ch, t).start()
+    def last_bands(ch):
         for t in (7, 1):
-            gather(ch, t).start()
-
-    def last_bands(ch):
-        for t in (7, 1, 5, 3, 4):
             gather(ch, t).wait_recv()
-            share(ch, t).start()
+        share(ch, 0).start()
+        share(ch, 1).start()
+        for t in (5, 3, 4):
+            gather(ch, t).wait_recv()
+        share(ch, 2).start()
 
     def back_z(ch):
-        for t in range(ring):
-            share(ch, t).wait_recv()
+        for part in range(3):
+            share(ch, part).wait_recv()
         for g in range(groups):
             spectral = d_in[ch, :, :, g * 16 : (g + 1) * 16].reshape(gz * 16, lanes)
             value = gelu_tanh(dot(spectral, table, ((0,), (0,))) + lin[ch, g])
@@ -391,8 +393,8 @@
         remote(
             d_in.at[ch, 0, others], d_in.at[ch, 0, others], d_s.at[ch], d_r.at[ch, 1], chip(1)
         ).wait_send()
-        for t in range(ring):
-            share(ch, t).wait_send()
+        for part in range(3):
+            share(ch, part).wait_send()
     remote(w_in.at[rest], w_in.at[rest], w_s, w_r, chip(1)).wait_send()
 
 
@@ -440,7 +442,7 @@
         dma((CHUNKS,)), dma((CHUNKS,)),
         dma((CHUNKS,)), dma((CHUNKS,)),
         dma((CHUNKS,)), dma((CHUNKS, ring)),
-        dma((CHUNKS, ring)), dma((CHUNKS, ring)),
+        dma((CHUNKS, 3)), dma((CHUNKS, 3)),
         dma, dma,
     ]
     anywhere = pl.BlockSpec(memory_space=pltpu.HBM)

time: 54.2 us -> 53.9 us (level)
  Pallas kernels: 52.7 us -> 52.1 us
    pallas_call x1, Pallas kernels: 52.7 us -> 52.1 us  [on_device(): pl.pallas_call(functools.partial(kernel, geometry, scale), out_shape=pltp...]
where the time goes in v5:
time: 53.9 us; the launch traced here: 53.4 us
  Pallas kernels  52.1 us (97%)
  local copies, waits for them, and re-layouts  1.32 us (2%)
    pallas_call x1, Pallas kernels, on_device(): pl.pallas_call(functools.partial(kernel, geometry, scale), out_shape=pltp...  52.1 us
    unnamed x1, local copies, waits for them, and re-layouts  1.32 us

profile of v5, /device:TPU:1, one launch (start us, length us, event | category | flops | bytes accessed | tf_op | source)
XLA Modules:
  0.0 53.4 jit_solution(14960942431031556174)
XLA Ops:
  0.0 52.1 %spectral_layer.1 = bf16[8,16,64,128]{3,2,1,0:T(8,128)(2,1)S(1)} custom-call(bf16[8,16,64,128]{3,2,1,0:T(8,128)(2,1)} %field.1, bf16[2,32,2,4,64]{4,3,2,1,0:T(4,128)(2,1)} %weight.1, bf16[64,64]{1,0:T(8,128)(2,1)} %pointwise_in.1, bf16[1,64]{1,0:T(2,128)(2,1)} %bitcast.1, f32[16,256,128]{2,1,0:T(8,128)} %constant.6.clone.table_z, ...), custom_call_target="tpu_custom_call" | custom-call | tf_op jit(solution)/shard_map/spectral_layer/pallas_call | solution.py:450
  52.1 1.3 %copy.9 = bf16[8,16,64,128]{3,2,1,0:T(8,128)(2,1)} copy(bf16[8,16,64,128]{3,2,1,0:T(8,128)(2,1)S(1)} %spectral_layer.1) | data formatting | bytes 4194304

commit v6 on v5

--- a/solution.py
+++ b/solution.py
@@ -124,12 +124,14 @@
     def to_sibling(ch):
         return remote(sib_out.at[ch], sib_in.at[ch], sib_s.at[ch], sib_r.at[ch], sibling)
 
+    place_of = {3: 0, 1: 1, 5: 2, 7: 3, 4: 4, 2: 5, 6: 6}
+
     def towards(ch, t):
-        target, place = {
-            1: (1, 0), 7: (7, 1), 2: (2, 2), 6: (6, 3), 3: (1, 4), 5: (7, 5), 4: (6 if ch % 2 else 2, 6)
-        }[t]
+        target = {3: 1, 5: 7, 4: 6 if ch % 2 else 2, 2: 2, 6: 6}[t]
+        place = place_of[t]
+        blocks = pl.ds(place, 2 if t in (3, 5) else 1)
         return remote(
-            a_out.at[ch, t - 1], a_in.at[ch, place], a_s.at[ch], a_r.at[ch, place], chip(target)
+            a_out.at[ch, blocks], a_in.at[ch, blocks], a_s.at[ch], a_r.at[ch, place], chip(target)
         )
 
     def weights_to(step):
@@ -236,11 +238,8 @@
             for t in (0, 2, 6):
                 acc[ch, g, t * 16 : (t + 1) * 16] = total[t * 16 : (t + 1) * 16]
             for t in (3, 4, 5, 1, 7):
-                a_out[ch, t - 1, g * 16 : (g + 1) * 16] = total[t * 16 : (t + 1) * 16].astype(BF16)
+                a_out[ch, place_of[t], g * 16 : (g + 1) * 16] = total[t * 16 : (t + 1) * 16].astype(BF16)
         for t in (4, 3, 5):
-            towards(ch, t).start()
-    for ch in chunks:
-        for t in (1, 7):
             towards(ch, t).start()
 
     get_mix.wait()
@@ -267,15 +266,15 @@
     for ch in chunks:
         for t in (3, 5, 4):
             towards(ch, t).wait_recv()
-        across = a_in[ch, 6].astype(F32)
-        right = own_sums(ch, 2) + a_in[ch, 4].astype(F32)
-        left = own_sums(ch, 6) + a_in[ch, 5].astype(F32)
+        across = a_in[ch, place_of[4]].astype(F32)
+        right = own_sums(ch, 2) + a_in[ch, place_of[3]].astype(F32)
+        left = own_sums(ch, 6) + a_in[ch, place_of[5]].astype(F32)
         if ch % 2:
             left = left + across
         else:
             right = right + across
-        a_out[ch, 1] = right.astype(BF16)
-        a_out[ch, 5] = left.astype(BF16)
+        a_out[ch, place_of[2]] = right.astype(BF16)
+        a_out[ch, place_of[6]] = left.astype(BF16)
         towards(ch, 2).start()
         towards(ch, 6).start()
 
@@ -283,11 +282,11 @@
     ahead = tf[...].astype(BF16)
     ahead = jnp.concatenate([ahead, ahead], axis=1)
     for ch in chunks:
-        for t in (1, 7, 2, 6):
+        for t in (2, 6):
             towards(ch, t).wait_recv()
         modes = own_sums(ch, 0)
-        for place in range(4):
-            modes = modes + a_in[ch, place].astype(F32)
+        for t in (1, 7, 2, 6):
+            modes = modes + a_in[ch, place_of[t]].astype(F32)
         high, low = split(modes)
         part = dot(ahead, jnp.concatenate([high, low], axis=0)).reshape(gy, 8, lanes)
         part = jnp.concatenate([part[:, :, h * 128 : (h + 1) * 128] for h in range(fold)], axis=1)

time: 53.9 us -> 53.5 us (level)
  no operation moved by 1% of the time
where the time goes in v6:
time: 53.5 us; the launch traced here: 53.4 us
  Pallas kernels  52.1 us (97%)
  local copies, waits for them, and re-layouts  1.32 us (2%)
    pallas_call x1, Pallas kernels, on_device(): pl.pallas_call(functools.partial(kernel, geometry, scale), out_shape=pltp...  52.1 us
    unnamed x1, local copies, waits for them, and re-layouts  1.32 us

profile of v6, /device:TPU:1, one launch (start us, length us, event | category | flops | bytes accessed | tf_op | source)
XLA Modules:
  0.0 53.4 jit_solution(3503189879005807706)
XLA Ops:
  0.0 52.1 %spectral_layer.1 = bf16[8,16,64,128]{3,2,1,0:T(8,128)(2,1)S(1)} custom-call(bf16[8,16,64,128]{3,2,1,0:T(8,128)(2,1)} %field.1, bf16[2,32,2,4,64]{4,3,2,1,0:T(4,128)(2,1)} %weight.1, bf16[64,64]{1,0:T(8,128)(2,1)} %pointwise_in.1, bf16[1,64]{1,0:T(2,128)(2,1)} %bitcast.1, f32[16,256,128]{2,1,0:T(8,128)} %constant.6.clone.table_z, ...), custom_call_target="tpu_custom_call" | custom-call | tf_op jit(solution)/shard_map/spectral_layer/pallas_call | solution.py:449
  52.1 1.3 %copy.9 = bf16[8,16,64,128]{3,2,1,0:T(8,128)(2,1)} copy(bf16[8,16,64,128]{3,2,1,0:T(8,128)(2,1)S(1)} %spectral_layer.1) | data formatting | bytes 4194304
